TPU v7x, 128 devices: a whole 4x4x4 slice. The times are simulated.
128 devices in a mesh: depth: 8 (over y_lo, z), rows: 2 (over core), cols: 8 (over x, y_hi).
Axes of the slice: x: 4, y: 4 (y_hi: 2, y_lo: 2; y = y_hi * 2 + y_lo), z: 4, core: 2. Of those that a mesh axis runs over, the one named last changes fastest.
Arguments:
- lower_panels: bfloat16 [16, 8, 768, 1024], P('depth', None, None, ('rows', 'cols')), may hold values from -0.23925781 to 0.23925781
- upper_panels: bfloat16 [16, 1024, 6144], P('depth', 'rows', 'cols'), may hold values from -0.23925781 to 0.23925781
- given_inverse: bfloat16 [16, 1024, 1024], P('depth', 'rows'), may hold values from -0.05625 to 2, as said below
- structure: int32 [16, 48], P('depth'), may hold values 0 or 1
- ancestor_entries: float32 [6144, 6144], P(('depth', 'rows'), 'cols'), may hold values from -0.6 to 19.2, as said below
Outputs:
- column_factor: float32 [6144, 512], P(('depth', 'rows'))
- trailing: float32 [6144, 6144], P(('depth', 'rows'), 'cols')
Inputs may be any that keep to these rules, and one draw needn't show every extreme that they name: `given_inverse`: off-diagonal entries are small against the diagonal. `ancestor_entries`: diagonal entries lie between 12.8 and 19.2.
All inputs are finite; a program needn't handle non-finite values. No bound on the sum of `structure` on one device may be relied on, other than what follows from the above.
Results may differ from a plain program's by a relative error of at most 0.0003.
Values may be sent and summed in bfloat16 or wider, within the bound.
A program may use at most 128 MiB of HBM per device.

v0:
```python
import jax
import jax.numpy as jnp
from jax import lax
from jax.sharding import PartitionSpec as P

PW = 512
NEWTON = 2


def from_root(array, axis, root):
    mine = lax.axis_index(axis) == root
    return lax.psum(jnp.where(mine, array, jnp.zeros_like(array)), axis)


def local(lower_panels, upper_panels, given_inverse, structure, ancestor_entries):
    highest = lax.Precision.HIGHEST
    subtree_count = lower_panels.shape[0]
    depth_count = lax.axis_size("depth")
    rows_count = lax.axis_size("rows")
    block_rows = lower_panels.shape[2]
    local_cols = upper_panels.shape[2]
    row_share = block_rows // rows_count
    block_count = structure.shape[1]
    block_size = depth_count * block_rows // block_count
    kept_blocks = (structure != 0).astype(jnp.bfloat16)
    lower_masked = (
        lower_panels.reshape(subtree_count, block_count, block_size, lower_panels.shape[3])
        * kept_blocks[:, :, None, None]
    ).reshape(lower_panels.shape)
    col_blocks = local_cols // block_size
    col_kept = lax.dynamic_slice_in_dim(
        kept_blocks, lax.axis_index("cols") * col_blocks, col_blocks, 1
    )
    upper_masked = (
        upper_panels.reshape(subtree_count, upper_panels.shape[1], col_blocks, block_size)
        * col_kept[:, None, :, None]
    ).reshape(upper_panels.shape)
    upper_full = lax.all_gather(upper_masked, "rows", axis=1, tiled=True)
    applied_half = jnp.einsum(
        "sik,skc->sic", given_inverse, upper_full, preferred_element_type=jnp.float32
    ).astype(jnp.bfloat16)
    update = jnp.einsum(
        "sjqk,skc->jqc",
        lax.all_gather(lower_masked, "cols", axis=3, tiled=True),
        applied_half,
        preferred_element_type=jnp.float32,
    )
    negated = (-update).reshape(depth_count * rows_count, row_share, local_cols)
    owned_sum = lax.psum_scatter(negated, ("depth", "rows"), scatter_dimension=0, tiled=True)[0]
    ancestor = ancestor_entries + owned_sum
    first_row = lax.axis_index(("depth", "rows")) * row_share
    row_offset = jnp.arange(PW, dtype=jnp.int32) - first_row
    inside = (row_offset >= 0) & (row_offset < row_share)
    picked = jnp.take(ancestor, jnp.clip(row_offset, 0, row_share - 1), axis=0)
    picked = jnp.where(inside[:, None], picked, jnp.zeros_like(picked))
    top_block = lax.psum(picked, ("depth", "rows"))
    column_panel, pivot = (
        from_root(ancestor[:, :PW], "cols", 0),
        from_root(top_block[:, :PW], "cols", 0),
    )
    identity = jnp.eye(PW, dtype=jnp.float32)
    inverse = identity / 16.0
    for sweep in range(NEWTON):
        product = jnp.dot(pivot, inverse, precision=highest)
        inverse = jnp.dot(inverse, 2.0 * identity - product, precision=highest)
    column_factor = jnp.dot(column_panel, inverse, precision=highest)
    trailing = ancestor - jnp.dot(column_factor, top_block, precision=highest)
    return (column_factor, trailing)


def solution(mesh):
    return jax.shard_map(
        local,
        mesh=mesh,
        in_specs=(
            P("depth", None, None, ("rows", "cols")),
            P("depth", "rows", "cols"),
            P("depth", "rows", None),
            P("depth", None),
            P(("depth", "rows"), "cols"),
        ),
        out_specs=(P(("depth", "rows"), None), P(("depth", "rows"), "cols")),
        check_vma=False,
    )
```

profile of v0, /device:TPU:0, one launch (start us, length us, event | category | flops | bytes accessed | tf_op | source)
XLA Modules:
  0.0 562.5 jit_solution(16396072703336000724)
XLA Ops:
  7.2 0.8 compare_convert_fusion
  8.1 0.1 constant_dynamic-slice_fusion
  8.1 0.1 broadcast_bitcast_fusion
  8.2 2.7 broadcast_multiply_fusion
  11.0 0.1 mul.41
  11.1 2.7 copy_multiply_fusion
  13.9 14.5 %all-gather.5.cloned.1.call-done = bf16[2,1024,768]{2,1,0:T(8,128)(2,1)} async-done(((bf16[2,512,768]{2,1,0:T(8,128)(2,1)}), bf16[2,1024,768]{2,1,0:T(8,128)(2,1)}) %all-gather.5.cloned.1.call-update) | async-done | bytes 3145744 | tf_op jit(solution)/shard_map/all_gather | solution.py:38
  28.3 151.1 %all-gather.3.cloned.1.call-done = bf16[2,8,768,512]{2,3,0,1:T(8,128)(2,1)} async-done(((bf16[2,8,768,64]{2,3,0,1:T(8,128)(2,1)}), bf16[2,8,768,512]{2,3,0,1:T(8,128)(2,1)}) %all-gather.3.cloned.1.call-update) | async-done | bytes 12582928 | tf_op jit(solution)/shard_map/all_gather | solution.py:44
  179.4 20.8 %bitcast_negate_fusion = f32[8,768,768]{2,1,0:T(8,128)} fusion(bf16[2,8,768,512]{2,3,0,1:T(8,128)(2,1)} %all-gather.3.cloned.1.call-done, bf16[2,512,1024]{2,1,0:T(8,128)(2,1)S(1)} %copy-done, bf16[2,1024,768]{2,1,0:T(8,128)(2,1)} %all-gather.5.cloned.1.call-done), kind=kOutput, calls=%fused_computation.1 | convolution fusion | flops 11279794176 | bytes 36700160 | tf_op jit(solution)/shard_map/sjqk,skc->jqc/dot_general | solution.py:42
  200.3 107.1 %reduce-scatter.2.cloned.1.call-done = f32[1,384,768]{2,1,0:T(8,128)} async-done(((f32[16,384,768]{2,1,0:T(8,128)}), f32[1,384,768]{2,1,0:T(8,128)}) %reduce-scatter.2.cloned.1.call-update) | async-done | bytes 1179664 | tf_op jit(solution)/shard_map/reduce_scatter | solution.py:49
  307.4 1.8 bitcast_add_fusion
  309.2 2.6 gather_fusion
  311.8 2.8 select_select_fusion
  314.6 0.2 all-reduce.6.cloned.1.call-start
  314.8 1.0 slice_select_fusion.1
  315.8 119.0 %all-reduce.4.cloned.1.call-done = f32[512,768]{1,0:T(8,128)} async-done(((f32[512,768]{1,0:T(8,128)}), f32[512,768]{1,0:T(8,128)}) %all-reduce.4.cloned.1.call-update) | async-done | bytes 1572880 | tf_op jit(solution)/shard_map/psum | solution.py:56
  434.8 2.3 slice_select_fusion
  437.1 105.7 %all-reduce.6.cloned.1.call-done = (f32[384,512]{1,0:T(8,128)}, f32[512,512]{1,0:T(8,128)}) async-done(((f32[384,512]{1,0:T(8,128)}, f32[512,512]{1,0:T(8,128)}), (f32[384,512]{1,0:T(8,128)}, f32[512,512]{1,0:T(8,128)})) %all-reduce.6.cloned.1.call-update) | async-done | bytes 1835024 | tf_op jit(solution)/shard_map/psum | solution.py:12
  542.8 3.0 select_subtract_fusion.1
  545.8 1.8 fusion.1
  547.7 1.9 select_subtract_fusion
  549.5 1.9 fusion.18
  551.4 1.4 fusion.19
  552.9 3.1 convolution_subtract_fusion
  (25 shorter events, 0.4 us)
Async XLA Ops:
  7.2 172.2 %copy-start = (bf16[2,512,1024]{2,1,0:T(8,128)(2,1)S(1)}, bf16[2,512,1024]{2,1,0:T(8,128)(2,1)}, u32[]{:S(2)}) copy-start(bf16[2,512,1024]{2,1,0:T(8,128)(2,1)} %param.7) | copy-start | bytes 6291460
  7.2 21.2 %all-gather.5.cloned.1.call-start = ((), (), s32[]{:S(2)}) async-start(), calls=%async_computation.2 | async-start | bytes 4718592 | tf_op jit(solution)/shard_map/all_gather | solution.py:38
  10.9 168.5 %all-gather.3.cloned.1.call-start = ((), (), s32[]{:S(2)}) async-start(), calls=%async_computation.1 | async-start | bytes 14155776 | tf_op jit(solution)/shard_map/all_gather | solution.py:44
  13.8 293.6 %reduce-scatter.2.cloned.1.call-start = ((), (), s32[]{:S(2)}) async-start(), calls=%async_computation.3 | async-start | bytes 20054016 | tf_op jit(solution)/shard_map/reduce_scatter | solution.py:49
  200.2 234.6 %all-reduce.4.cloned.1.call-start = ((), (), s32[]{:S(2)}) async-start(), calls=%async_computation.4 | async-start | bytes 3145728 | tf_op jit(solution)/shard_map/psum | solution.py:56
  314.6 228.2 %all-reduce.6.cloned.1.call-start = ((), (), s32[]{:S(2)}) async-start(), calls=%async_computation.5 | async-start | bytes 3670016 | tf_op jit(solution)/shard_map/psum | solution.py:12
  545.8 1.8 copy-start.3
  549.5 1.9 copy-start.4
  551.4 1.5 copy-start.1
  552.9 3.1 copy-start.2
Sparse Core Ops, SparseCore 0:
  11.0 17.2 all-gather.4
  30.7 148.6 all-gather.2
  200.3 107.0 reduce-scatter.1
  314.7 120.0 all-reduce.3
  438.0 104.7 all-reduce.5
where the time goes:
time: 563 us
  waiting for transfers between devices  497 us (88%)
  matrix products  33.9 us (6%)
  other arithmetic  14 us (2%)
  between operations  13.9 us (2%)
    all_gather x1, waiting for transfers between devices, local(): lax.all_gather(lower_masked, 'cols', axis=3, tiled=True)  151 us
    psum x1, waiting for transfers between devices, local(): top_block = lax.psum(picked, ('depth', 'rows'))  119 us
    reduce_scatter x1, waiting for transfers between devices, local(): lax.psum_scatter(negated, ('depth', 'rows'), scatter_dimension=0, tiled=T...  107 us
    psum x1, waiting for transfers between devices, from_root(): return lax.psum(jnp.where(mine, array, jnp.zeros_like(array)), axis)  106 us
    dot_general x1, matrix products, local(): jnp.einsum('sjqk,skc->jqc', lax.all_gather(lower_masked, 'cols', axis=3,...  20.8 us
    all_gather x1, waiting for transfers between devices, local(): upper_full = lax.all_gather(upper_masked, 'rows', axis=1, tiled=True)  14.5 us
  transfers between devices with their start and end apart: 5, of which 5 were waited for; matrix products, arithmetic and copies ran while one was open for 1% of the time, Pallas kernels for 0%

commit v1 on v0

--- a/solution.py
+++ b/solution.py
@@ -35,7 +35,9 @@
         upper_panels.reshape(subtree_count, upper_panels.shape[1], col_blocks, block_size)
         * col_kept[:, None, :, None]
     ).reshape(upper_panels.shape)
-    upper_full = lax.all_gather(upper_masked, "rows", axis=1, tiled=True)
+    upper_full = jnp.concatenate(
+        lax.all_to_all(jnp.stack([upper_masked] * lax.axis_size("rows")), "rows", 0, 0), axis=1
+    )
     applied_half = jnp.einsum(
         "sik,skc->sic", given_inverse, upper_full, preferred_element_type=jnp.float32
     ).astype(jnp.bfloat16)

time: 563 us -> 543 us (0.964)
  waiting for transfers between devices: 497 us -> 472 us
  blocking collectives: 0 us -> 6.26 us
    all_gather x1 -> x0, waiting for transfers between devices: 14.5 us -> none  [local(): upper_full = lax.all_gather(upper_masked, 'rows', axis=1, tiled=True)]
    all_gather x1, waiting for transfers between devices: 151 us -> 140 us  [local(): lax.all_gather(lower_masked, 'cols', axis=3, tiled=True)]
    all_to_all x0 -> x1, blocking collectives: none -> 6.26 us  [local(): lax.all_to_all(jnp.stack([upper_masked] * lax.axis_size('rows')), 'rows',...]
  transfers between devices with their start and end apart: 5 -> 4, of which waited for: 5 -> 4; matrix products, arithmetic and copies ran while one was open for 1% -> 1% of each run, Pallas kernels for 0% -> 0%
where the time goes in v1:
time: 543 us
  waiting for transfers between devices  472 us (87%)
  matrix products  34.8 us (6%)
  between operations  14 us (3%)
  other arithmetic  11.4 us (2%)
  blocking collectives  6.26 us (1%)
    all_gather x1, waiting for transfers between devices, local(): lax.all_gather(lower_masked, 'cols', axis=3, tiled=True)  140 us
    psum x1, waiting for transfers between devices, local(): top_block = lax.psum(picked, ('depth', 'rows'))  119 us
    reduce_scatter x1, waiting for transfers between devices, local(): lax.psum_scatter(negated, ('depth', 'rows'), scatter_dimension=0, tiled=T...  107 us
    psum x1, waiting for transfers between devices, from_root(): return lax.psum(jnp.where(mine, array, jnp.zeros_like(array)), axis)  106 us
    dot_general x1, matrix products, local(): jnp.einsum('sjqk,skc->jqc', lax.all_gather(lower_masked, 'cols', axis=3,...  21.7 us
  transfers between devices with their start and end apart: 4, of which 4 were waited for; matrix products, arithmetic and copies ran while one was open for 1% of the time, Pallas kernels for 0%

profile of v1, /device:TPU:0, one launch (start us, length us, event | category | flops | bytes accessed | tf_op | source)
XLA Modules:
  0.0 542.7 jit_solution(9886980977338587647)
XLA Ops:
  7.2 0.8 compare_convert_fusion
  8.0 0.1 mul.44
  8.2 2.7 copy_multiply_fusion
  11.1 1.5 multiply_bitcast_fusion
  12.7 0.3 pad_maximum_fusion
  12.9 6.3 %all_to_all.5 = bf16[2,2,512,768]{3,2,1,0:T(8,128)(2,1)S(1)} all-to-all(bf16[2,2,512,768]{3,2,1,0:T(8,128)(2,1)S(1)} %pad_maximum_fusion), channel_id=1, replica_groups=mesh['depth'=8,'rows'=2,'cols'=8] {'rows'}, dimensions={0} | all-to-all | bytes 6291456 | tf_op jit(solution)/shard_map/all_to_all | solution.py:39
  19.2 1.8 copy.12
  21.0 139.8 %all-gather.2.cloned.1.call-done = bf16[2,8,768,512]{2,3,0,1:T(8,128)(2,1)} async-done(((bf16[2,8,768,64]{2,3,0,1:T(8,128)(2,1)}), bf16[2,8,768,512]{2,3,0,1:T(8,128)(2,1)}) %all-gather.2.cloned.1.call-update) | async-done | bytes 12582928 | tf_op jit(solution)/shard_map/all_gather | solution.py:46
  160.9 21.7 %bitcast_negate_fusion = f32[8,768,768]{2,1,0:T(8,128)} fusion(bf16[2,8,768,512]{2,3,0,1:T(8,128)(2,1)} %all-gather.2.cloned.1.call-done, bf16[2,1024,768]{2,1,0:T(8,128)(2,1)} %bitcast.44, bf16[2,512,1024]{2,1,0:T(8,128)(2,1)S(1)} %copy-done), kind=kOutput, calls=%fused_computation.1 | convolution fusion | flops 11279794176 | bytes 36700160 | tf_op jit(solution)/shard_map/sjqk,skc->jqc/dot_general | solution.py:44
  182.7 107.1 %reduce-scatter.2.cloned.1.call-done = f32[1,384,768]{2,1,0:T(8,128)} async-done(((f32[16,384,768]{2,1,0:T(8,128)}), f32[1,384,768]{2,1,0:T(8,128)}) %reduce-scatter.2.cloned.1.call-update) | async-done | bytes 1179664 | tf_op jit(solution)/shard_map/reduce_scatter | solution.py:51
  289.8 1.4 bitcast_add_fusion
  291.2 1.9 gather_fusion
  293.1 1.4 select_select_fusion
  294.5 0.2 all-reduce.6.cloned.1.call-start
  294.7 1.0 slice_select_fusion.1
  295.7 119.0 %all-reduce.4.cloned.1.call-done = f32[512,768]{1,0:T(8,128)} async-done(((f32[512,768]{1,0:T(8,128)}), f32[512,768]{1,0:T(8,128)}) %all-reduce.4.cloned.1.call-update) | async-done | bytes 1572880 | tf_op jit(solution)/shard_map/psum | solution.py:58
  414.7 2.3 slice_select_fusion
  417.0 105.9 %all-reduce.6.cloned.1.call-done = (f32[384,512]{1,0:T(8,128)}, f32[512,512]{1,0:T(8,128)}) async-done(((f32[384,512]{1,0:T(8,128)}, f32[512,512]{1,0:T(8,128)}), (f32[384,512]{1,0:T(8,128)}, f32[512,512]{1,0:T(8,128)})) %all-reduce.6.cloned.1.call-update) | async-done | bytes 1835024 | tf_op jit(solution)/shard_map/psum | solution.py:12
  522.9 3.0 select_subtract_fusion.1
  525.9 1.8 fusion.1
  527.8 1.9 select_subtract_fusion
  529.6 1.8 fusion.18
  531.5 1.4 fusion.19
  533.0 3.1 convolution_subtract_fusion
  (29 shorter events, 0.5 us)
Async XLA Ops:
  7.2 153.7 %copy-start = (bf16[2,512,1024]{2,1,0:T(8,128)(2,1)S(1)}, bf16[2,512,1024]{2,1,0:T(8,128)(2,1)}, u32[]{:S(2)}) copy-start(bf16[2,512,1024]{2,1,0:T(8,128)(2,1)} %param.7) | copy-start | bytes 6291460
  7.2 153.7 %all-gather.2.cloned.1.call-start = ((), (), s32[]{:S(2)}) async-start(), calls=%async_computation.2 | async-start | bytes 14155776 | tf_op jit(solution)/shard_map/all_gather | solution.py:46
  10.9 278.9 %reduce-scatter.2.cloned.1.call-start = ((), (), s32[]{:S(2)}) async-start(), calls=%async_computation.3 | async-start | bytes 20054016 | tf_op jit(solution)/shard_map/reduce_scatter | solution.py:51
  182.6 107.2 %copy-start.4 = (f32[384,768]{1,0:T(8,128)S(1)}, f32[384,768]{1,0:T(8,128)}, u32[]{:S(2)}) copy-start(f32[384,768]{1,0:T(8,128)} %param.9) | copy-start | bytes 3538948
  182.6 232.1 %all-reduce.4.cloned.1.call-start = ((), (), s32[]{:S(2)}) async-start(), calls=%async_computation.4 | async-start | bytes 3145728 | tf_op jit(solution)/shard_map/psum | solution.py:58
  294.5 228.4 %all-reduce.6.cloned.1.call-start = ((), (), s32[]{:S(2)}) async-start(), calls=%async_computation.5 | async-start | bytes 3670016 | tf_op jit(solution)/shard_map/psum | solution.py:12
  525.9 1.8 copy-start.5
  529.6 1.9 copy-start.6
  531.5 1.5 copy-start.2
  531.5 4.6 copy-start.1
  533.0 3.1 copy-start.3
Sparse Core Ops, SparseCore 0:
  11.0 149.7 all-gather.1
  182.7 107.0 reduce-scatter.1
  294.6 120.0 all-reduce.3
  417.9 104.9 all-reduce.5
